TPU v7x, 256 devices: a whole 4x4x8 slice. The times are simulated.
256 devices in a mesh: box: 64 (over z, x, core), rhs: 4 (over y).
Axes of the slice: x: 4, y: 4, z: 8, core: 2. Of those that a mesh axis runs over, the one named last changes fastest.
Arguments:
- leaf_coords: float32 [3, 131072], P(None, 'box'), may hold values from -6 to 6
- charges: float32 [32, 131072], P('rhs', 'box'), may hold values from -6 to 6
- leaf_skeleton: float32 [3, 32768], P(None, 'box'), may hold values from -6 to 6
- parent_skeleton: float32 [3, 4096], P(None, 'box'), may hold values from -6 to 6
- interp: float32 [512, 64, 256], P(('box', 'rhs')), may hold values from -0.375 to 0.375
- transfer: float32 [64, 64, 512], P('box'), may hold values from -0.25 to 0.25
- near_offset: int32 [5120, 1], replicated, may hold values from 0 to 6; in each aligned block of 80 rows (0 to 79, 80 to 159, ...) at most 16 rows name the same one
- near_partner: int32 [5120], replicated, may hold values from 0 to 7
- near_count: int32 [64], replicated, may hold values from 1 to 80, 3200 in all
- far_offset: int32 [6912, 1], replicated, may hold values from 0 to 6; in each aligned block of 108 rows (0 to 107, 108 to 215, ...) at most 21 rows name the same one
- far_partner: int32 [6912], replicated, may hold values from 0 to 8, as said below
Outputs:
- potential: float32 [32, 131072], P('rhs', 'box')
Inputs may be any that keep to these rules, and one draw needn't show every extreme that they name: `near_offset`: the partner of a pair lies at owner index (own index + offset - 3) mod the number of indices of box. In each device's block of 80 rows at most 16 rows name one offset, and some offset is named by exactly that many in some block. `near_count`: live rows of each block are its first ones; some block is fully live. `far_offset`: in each device's block of 108 rows at most 21 rows name one offset, and some offset is named by exactly that many in some block. `far_partner`: rows of a leaf entry name a leaf (below 8); rows of a parent entry name a parent (from 8 on).
All inputs are finite; a program needn't handle non-finite values.
Results may differ from a plain program's by a relative error of at most 0.0001.
Values sent between devices are 32-bit elements; how exact they have to be, the bound alone decides.
A program may use at most 64 MiB of HBM per device.

v0:
```python
import functools

import jax
import jax.numpy as jnp
from jax import lax
from jax.experimental import pallas as pl
from jax.experimental.pallas import tpu as pltpu
from jax.sharding import PartitionSpec as P

REACH = 3
SPAN = 2 * REACH + 1
SOFTEN = 0.0025
COUPLE = 0.07957747154594767

LEAF = 256
SKEL = 64
LEAVES = 8
COLS = 8
NEAR_PER = 10
FAR_PER = 12
ENTRIES = 9
NEAR_ROWS = LEAVES * NEAR_PER
FAR_ROWS = ENTRIES * FAR_PER
TABLE = 640

MESH = pl.DeviceIdType.MESH
NN = (((1,), (0,)), ((), ()))
NT = (((1,), (1,)), ((), ()))
f32, bf16, i32 = jnp.float32, jnp.bfloat16, jnp.int32


def split(value):
    high = value.astype(bf16)
    low = (value - high.astype(f32)).astype(bf16)
    return high, low


def stacked(value):
    return jnp.concatenate(split(value), axis=0)


def folded(value):
    return value[:8] + value[8:16]


def mul(a, b, dims=NN):
    return lax.dot_general(a, b, dims, preferred_element_type=f32)


def lane_index(shape):
    return lax.broadcasted_iota(i32, shape, 1)


def row_index(shape):
    return lax.broadcasted_iota(i32, shape, 0)


def column_form(row, width):
    return jnp.transpose(jnp.broadcast_to(row, (128, width)))


def inverse_distance(ax, ay, az, bx, by, bz):
    dx, dy, dz = ax - bx, ay - by, az - bz
    return lax.rsqrt((dx * dx + SOFTEN) + (dy * dy + dz * dz))


def tile_pieces(spread, leaf, points, high, low):
    def piece(c):
        s = pl.ds(c * 32, 32)
        for h in range(2):
            at = slice(h * 128, h * 128 + 128)
            k = inverse_distance(
                spread[0, leaf, s, :], spread[1, leaf, s, :], spread[2, leaf, s, :],
                points[0:1, at], points[1:2, at], points[2:3, at],
            )
            high[s, at], low[s, at] = split(k)

    return [functools.partial(piece, c) for c in range(8)]


def interleave(first, second):
    each = max(1, -(-len(second) // max(1, len(first))))
    for j, step in enumerate(first):
        step()
        for other in second[j * each:(j + 1) * each]:
            other()
    for other in second[len(first) * each:]:
        other()


def kernel(
    boxes, sides,
    coords, charges, leaf_skel, parent_skel, interp, transfer,
    near_offset, near_partner, near_count, far_offset, far_partner,
    out,
    vals, pts, skel, tables, near_send, near_recv, far_send, far_recv, gathered,
    spread, spread_skel, own_v, kh0, kh1, kl0, kl1, near_x0, near_x1, own_sum,
    left_t, right_t, k_far, v_far, far_x, far_own, far_mat, ih, il, near_sum, far_sum,
    s_int, r_int, s_dat, r_dat, s_tab, r_tab, s_near, r_near, s_far, r_far,
):
    me = lax.axis_index("box")
    side = lax.axis_index("rhs")
    others = [o for o in range(SPAN) if o != REACH]

    def box_at(step):
        return lax.rem(me + (step + boxes), boxes)

    def side_at(step):
        return lax.rem(side + step, sides)

    barrier = pltpu.get_barrier_semaphore()
    for o in others:
        pl.semaphore_signal(barrier, inc=1, device_id={"box": box_at(o - REACH)}, device_id_type=MESH)
    for j in range(1, sides):
        pl.semaphore_signal(barrier, inc=1, device_id={"rhs": side_at(j)}, device_id_type=MESH)

    for leaf in range(LEAVES):
        at = slice(leaf * LEAF, (leaf + 1) * LEAF)
        own_v[leaf] = stacked(charges[:, at])
        for d in range(3):
            spread[d, leaf] = column_form(coords[d:d + 1, at], LEAF)
        vals[REACH, leaf] = charges[:, at]
        pts[REACH, leaf] = coords[:, at]
    for d in range(3):
        spread_skel[d, :LEAVES * SKEL] = column_form(leaf_skel[d:d + 1, :], LEAVES * SKEL)
        spread_skel[d, LEAVES * SKEL:] = column_form(parent_skel[d:d + 1, :], SKEL)
    skel[REACH, :, :512] = leaf_skel[...]
    skel[REACH, :, 512:] = jnp.concatenate([parent_skel[...], parent_skel[...]], axis=1)
    gathered[side] = interp[...]

    pl.semaphore_wait(barrier, len(others) + sides - 1)

    def remote(src, dst, send, recv, device):
        copy = pltpu.make_async_remote_copy(
            src_ref=src, dst_ref=dst, send_sem=send, recv_sem=recv, device_id=device, device_id_type=MESH
        )
        copy.start()
        return copy

    interp_copies = [
        remote(interp, gathered.at[side], s_int.at[j - 1], r_int.at[j - 1], {"rhs": side_at(j)})
        for j in range(1, sides)
    ]
    data_copies = []
    for o in (2, 4, 1, 5, 0, 6):
        target = {"box": box_at(REACH - o)}
        for n, src in enumerate((vals, pts, skel)):
            data_copies.append(remote(src.at[REACH], src.at[o], s_dat.at[n, o], r_dat.at[n, o], target))

    def self_pair(t, carry):
        buffers = ((kh0, kl0), (kh1, kl1))

        def matmuls(u):
            leaf = t * 2 + u
            high, low = buffers[u]

            def one():
                v = own_v[leaf]
                own_sum[leaf] = folded(mul(v, high[...], NT) + mul(v, low[...], NT))

            return [one]

        for u in range(2):
            leaf = t * 2 + u
            points = pts[REACH, leaf]
            for step in tile_pieces(spread, leaf, points, *buffers[u]):
                step()
        for u in range(2):
            matmuls(u)[0]()
        return carry

    lax.fori_loop(0, LEAVES // 2, self_pair, 0)

    left = lane_index((8, 128)) < SKEL
    for copy in interp_copies:
        copy.wait_recv()
    for m in range(4):
        high, low = split(gathered[m].reshape(128, LEAF))
        ih[m], il[m] = high, low
        both = jnp.concatenate([own_v[2 * m], own_v[2 * m + 1]], axis=0)
        got = mul(both, high, NT) + mul(both, low, NT)
        tables[REACH, :, m * 128:(m + 1) * 128] = jnp.where(left, folded(got[:16]), folded(got[16:]))
    t_high, t_low = split(transfer[0])
    children = stacked(tables[REACH, :, :LEAVES * SKEL])
    parents = folded(mul(children, t_high, NT) + mul(children, t_low, NT))
    tables[REACH, :, 512:576] = parents
    tables[REACH, :, 576:640] = jnp.zeros((COLS, SKEL), f32)
    table_copies = [
        remote(tables.at[REACH], tables.at[o], s_tab.at[o], r_tab.at[o], {"box": box_at(REACH - o)})
        for o in (2, 4, 1, 5, 0, 6)
    ]

    for copy in data_copies:
        copy.wait_recv()

    alive = near_count[me]
    near_base = me * NEAR_ROWS

    def near_leaf(leaf, carry):
        v_own = own_v[leaf]
        total = [own_sum[leaf]]
        highs, lows = (kh0, kh1), (kl0, kl1)

        def place(u):
            k = near_base + leaf * NEAR_PER + u
            return near_offset[k], near_partner[k]

        def tile(u):
            o, at = place(u)
            return tile_pieces(spread, leaf, pts[o, at], highs[u % 2], lows[u % 2])

        def matmuls(u):
            high, low = highs[u % 2], lows[u % 2]
            kept = {}

            def start():
                o, at = place(u)
                weight = jnp.where(leaf * NEAR_PER + u < alive, 1.0, 0.0).astype(f32)
                kept["v"] = stacked(vals[o, at] * weight)
                kept["other"] = mul(v_own, high[...])

            def second():
                other = folded(kept["other"] + mul(v_own, low[...]))
                at = pl.ds(pl.multiple_of((leaf * NEAR_PER + u) * 8, 8), 8)
                near_x0[at, :] = other[:, :128]
                near_x1[at, :] = other[:, 128:]

            def third():
                kept["own"] = mul(kept["v"], high[...], NT)

            def fourth():
                total[0] = total[0] + folded(kept["own"] + mul(kept["v"], low[...], NT))

            return [start, second, third, fourth]

        for step in tile(0):
            step()
        for u in range(NEAR_PER):
            interleave(matmuls(u), tile(u + 1) if u + 1 < NEAR_PER else [])
        own_sum[leaf] = total[0]
        return carry

    lax.fori_loop(0, LEAVES, near_leaf, 0)

    lanes = lane_index((1, 128))
    near_key = jnp.full((1, 128), -1, i32)
    for k in range(NEAR_ROWS):
        key = near_offset[near_base + k] * 8 + near_partner[near_base + k]
        near_key = jnp.where(lanes == k, jnp.where(k < alive, key, -1), near_key)
    chosen = jnp.where(row_index((64, 128)) == near_key, 1.0, 0.0).astype(bf16)[:, :NEAR_ROWS]
    for r in range(COLS):
        rows = pl.ds(r, NEAR_ROWS, stride=8)
        high, low = split(jnp.concatenate([near_x0[rows, :], near_x1[rows, :]], axis=1))
        reply = mul(chosen, high) + mul(chosen, low)
        for o in range(SPAN):
            for h in range(2):
                near_send[o, (2 * r + h) * 8:(2 * r + h + 1) * 8, :] = reply[8 * o:8 * o + 8, h * 128:h * 128 + 128]
    near_copies = [
        remote(near_send.at[o], near_recv.at[o], s_near.at[o], r_near.at[o], {"box": box_at(o - REACH)})
        for o in (0, 6, 1, 5, 2, 4)
    ]

    for copy in table_copies:
        copy.wait_recv()
    left3 = lane_index((3, 128)) < SKEL

    def halves(block, mask):
        turned = pltpu.roll(block, SKEL, 1)
        zero = jnp.zeros_like(block)
        even = (jnp.where(mask, block, zero), jnp.where(mask, zero, turned))
        odd = (jnp.where(mask, turned, zero), jnp.where(mask, zero, block))
        return even, odd

    def put(slot, value_pair, point_pair):
        for table, value, point in zip((left_t, right_t), value_pair, point_pair):
            table[slot, 0:8, :] = value
            table[slot, 8:11, :] = point

    for o in range(SPAN):
        for m in range(4):
            at = slice(m * 128, (m + 1) * 128)
            values = halves(tables[o, :, at], left)
            points = halves(skel[o, :, at], left3)
            for u in range(2):
                put(o * ENTRIES + 2 * m + u, values[u], points[u])
        values = halves(tables[o, :, 512:640], left)
        points = halves(skel[o, :, 512:640], left3)
        put(o * ENTRIES + LEAVES, values[0], points[0])

    far_base = me * FAR_ROWS

    def far_slot(k):
        return far_offset[far_base + k] * ENTRIES + far_partner[far_base + k]

    def far_entry(e, carry):
        mine = left_t[REACH * ENTRIES + e, 0:8, :] + right_t[REACH * ENTRIES + e, 0:8, :]
        v_own = stacked(mine)
        rows = pl.ds(pl.multiple_of(e * SKEL, SKEL), SKEL)
        for j in range(FAR_PER // 2):
            at = slice(j * 128, (j + 1) * 128)
            k = e * FAR_PER + 2 * j
            block = left_t[far_slot(k), 0:11, :] + right_t[far_slot(k + 1), 0:11, :]
            tile = inverse_distance(
                spread_skel[0, rows, :], spread_skel[1, rows, :], spread_skel[2, rows, :],
                block[8:9], block[9:10], block[10:11],
            )
            k_far[0:SKEL, at], k_far[SKEL:, at] = split(tile)
            v_far[:, at] = stacked(block[0:8])
        tiles = k_far[...]
        other = folded(mul(v_own, tiles))
        for j in range(FAR_PER // 2):
            at = pl.ds(pl.multiple_of((e * (FAR_PER // 2) + j) * 8, 8), 8)
            far_x[at, :] = other[:, j * 128:(j + 1) * 128]
        own = folded(mul(v_far[...], tiles, NT))
        far_own[e] = own + pltpu.roll(own, SKEL, 1)
        return carry

    lax.fori_loop(0, ENTRIES, far_entry, 0)

    pairs = FAR_ROWS // 2
    far_x[pairs * 8:, :] = jnp.zeros((512 - pairs * 8, 128), f32)
    keys = []
    for u in range(2):
        key_row = jnp.full((1, 128), -1, i32)
        for j in range(pairs):
            o, p = far_offset[far_base + 2 * j + u], far_partner[far_base + 2 * j + u]
            key = jnp.where(p < LEAVES, o * 8 + p, 8 * SPAN + o)
            key_row = jnp.where((lanes == j) | (lanes == j + 64), key, key_row)
        keys.append(jnp.where(row_index((64, 128)) == key_row, 1.0, 0.0).astype(bf16))
    chosen = jnp.concatenate(keys, axis=0)
    for r in range(COLS):
        high, low = split(far_x[pl.ds(r, 64, stride=8), :])
        far_mat[0:64, r * 128:(r + 1) * 128] = high
        far_mat[64:128, r * 128:(r + 1) * 128] = low
    reply = mul(chosen, far_mat[...])
    left64 = lane_index((64, 128)) < SKEL
    for m in range(4):
        a, b = slice(m * 128, (m + 1) * 128), slice((m + 4) * 128, (m + 5) * 128)
        straight = jnp.where(left64, reply[:64, a], reply[64:, b])
        crossed = jnp.where(left64, reply[:64, b], reply[64:, a])
        whole = straight + pltpu.roll(crossed, SKEL, 1)
        for o in range(SPAN):
            far_send[o, :, a] = whole[8 * o:8 * o + 8]
            far_send[o, m:m + 1, 512:640] = whole[8 * SPAN + o:8 * SPAN + o + 1]
    for o in range(SPAN):
        far_send[o, 4:8, 512:640] = jnp.zeros((4, 128), f32)
    far_copies = [
        remote(far_send.at[o], far_recv.at[o], s_far.at[o], r_far.at[o], {"box": box_at(o - REACH)})
        for o in (0, 6, 1, 5, 2, 4)
    ]

    for copy in far_copies:
        copy.wait_recv()
    total = far_send[REACH]
    for o in others:
        total = total + far_recv[o]
    for m in range(4):
        far_sum[m * 8:(m + 1) * 8, :] = total[:, m * 128:(m + 1) * 128]
    fours = total[0:4, 512:640]
    parent = jnp.concatenate([fours, pltpu.roll(fours, SKEL, 1)], axis=0) + far_own[LEAVES]
    parent = stacked(parent[:, :SKEL])
    handed = folded(mul(parent, t_high) + mul(parent, t_low))
    parts = []
    for m in range(4):
        down = handed[:, m * 128:(m + 1) * 128]
        even = far_sum[pl.ds(2 * m, 4, stride=8), :]
        odd = far_sum[pl.ds(2 * m + 1, 4, stride=8), :]
        even = jnp.concatenate([even, pltpu.roll(even, SKEL, 1)], axis=0) + far_own[2 * m] + down
        odd = jnp.concatenate([pltpu.roll(odd, SKEL, 1), odd], axis=0) + far_own[2 * m + 1] + down
        zero = jnp.zeros_like(even)
        both = jnp.concatenate([stacked(jnp.where(left, even, zero)), stacked(jnp.where(left, zero, odd))], axis=0)
        got = mul(both, ih[m]) + mul(both, il[m])
        parts += [folded(got[:16]), folded(got[16:])]

    for copy in near_copies:
        copy.wait_recv()
    total = near_send[REACH]
    for o in others:
        total = total + near_recv[o]
    near_sum[...] = total
    for leaf in range(LEAVES):
        for h in range(2):
            mine = slice(h * 128, (h + 1) * 128)
            arrived = near_sum[pl.ds(h * 8 + leaf, 8, stride=16), :]
            value = own_sum[leaf, :, mine] + arrived + parts[leaf][:, mine]
            out[:, leaf * LEAF + h * 128:leaf * LEAF + (h + 1) * 128] = COUPLE * value

    for copy in interp_copies + data_copies + table_copies + near_copies + far_copies:
        copy.wait_send()


def shards(
    leaf_coords, charges, leaf_skeleton, parent_skeleton, interp, transfer,
    near_offset, near_partner, near_count, far_offset, far_partner,
):
    boxes, sides = lax.axis_size("box"), lax.axis_size("rhs")
    vmem, smem = pl.BlockSpec(memory_space=pltpu.VMEM), pl.BlockSpec(memory_space=pltpu.SMEM)
    V, S = pltpu.VMEM, pltpu.SemaphoreType.DMA
    return pl.pallas_call(
        functools.partial(kernel, boxes, sides),
        out_shape=jax.ShapeDtypeStruct(charges.shape, f32),
        in_specs=[vmem] * 6 + [smem] * 5,
        out_specs=vmem,
        scratch_shapes=[
            V((SPAN, LEAVES, COLS, LEAF), f32),
            V((SPAN, LEAVES, 3, LEAF), f32),
            V((SPAN, 3, TABLE), f32),
            V((SPAN, COLS, TABLE), f32),
            V((SPAN, 128, 128), f32),
            V((SPAN, 128, 128), f32),
            V((SPAN, 8, TABLE), f32),
            V((SPAN, 8, TABLE), f32),
            V((4, 2, SKEL, LEAF), f32),
            V((3, LEAVES, LEAF, 128), f32),
            V((3, ENTRIES * SKEL, 128), f32),
            V((LEAVES, 16, LEAF), bf16),
            V((LEAF, LEAF), bf16),
            V((LEAF, LEAF), bf16),
            V((LEAF, LEAF), bf16),
            V((LEAF, LEAF), bf16),
            V((NEAR_ROWS * 8, 128), f32),
            V((NEAR_ROWS * 8, 128), f32),
            V((LEAVES, 8, LEAF), f32),
            V((64, 16, 128), f32),
            V((64, 16, 128), f32),
            V((128, FAR_PER * SKEL), bf16),
            V((16, FAR_PER * SKEL), bf16),
            V((512, 128), f32),
            V((ENTRIES, 8, 128), f32),
            V((128, 1024), bf16),
            V((4, 128, LEAF), bf16),
            V((4, 128, LEAF), bf16),
            V((128, 128), f32),
            V((32, 128), f32),
            S((3,)), S((3,)), S((3, SPAN)), S((3, SPAN)), S((SPAN,)), S((SPAN,)),
            S((SPAN,)), S((SPAN,)), S((SPAN,)), S((SPAN,)),
        ],
        compiler_params=pltpu.CompilerParams(
            collective_id=0, has_side_effects=True, vmem_limit_bytes=32 * 2**20
        ),
    )(
        leaf_coords, charges, leaf_skeleton, parent_skeleton, interp, transfer,
        near_offset.reshape(-1), near_partner, near_count, far_offset.reshape(-1), far_partner,
    )


def solution(mesh):
    return jax.shard_map(
        shards,
        mesh=mesh,
        in_specs=(
            P(None, "box"),
            P("rhs", "box"),
            P(None, "box"),
            P(None, "box"),
            P(("box", "rhs"), None, None),
            P("box", None, None),
            P(),
            P(),
            P(),
            P(),
            P(),
        ),
        out_specs=P("rhs", "box"),
        check_vma=False,
    )
```

profile of v0, /device:TPU:1, one launch (start us, length us, event | category | flops | bytes accessed | tf_op | source)
XLA Modules:
  0.0 54.6 jit_solution(15206879894137931551)
XLA Ops:
  0.0 0.0 copy-start.3
  0.0 0.0 copy-start.5
  0.0 0.0 copy-start.8
  0.0 0.0 copy-start.9
  0.0 0.9 %reduce.far_offset = s32[6912]{0:T(1024)S(1)} reduce(s32[6912,1]{0,1:T(1,128)} %param.20, s32[]{:T(128)} %constant.2), dimensions={1}, to_apply=%param.20.reduce_sub_computation | reduce | bytes 55300 | tf_op args[9]
  0.9 0.0 copy-done.3
  0.9 0.0 copy-done.5
  0.9 0.0 copy-done.8
  0.9 0.0 copy-done.9
  0.9 0.0 copy-start
  0.9 0.9 %copy-done = f32[2,64,256]{2,1,0:T(8,128)S(1)} copy-done((f32[2,64,256]{2,1,0:T(8,128)S(1)}, f32[2,64,256]{2,1,0:T(8,128)}, u32[]{:S(2)}) %copy-start) | copy-done | bytes 131096
  1.8 0.0 copy-start.1
  1.8 0.9 %copy-done.1 = f32[1,64,512]{2,1,0:T(8,128)S(1)} copy-done((f32[1,64,512]{2,1,0:T(8,128)S(1)}, f32[1,64,512]{2,1,0:T(8,128)}, u32[]{:S(2)}) %copy-start.1) | copy-done | bytes 131096
  2.7 0.0 copy-start.2
  2.7 0.8 %copy-done.2 = f32[8,2048]{1,0:T(8,128)S(1)} copy-done((f32[8,2048]{1,0:T(8,128)S(1)}, f32[8,2048]{1,0:T(8,128)}, u32[]{:S(2)}) %copy-start.2) | copy-done | bytes 65560
  3.6 0.0 copy-start.4
  3.6 0.7 %copy-done.4 = s32[6912]{0:T(1024)S(1)} copy-done((s32[6912]{0:T(1024)S(1)}, s32[6912]{0:T(1024)}, u32[]{:S(2)}) %copy-start.4) | copy-done | bytes 27672
  4.3 0.0 copy-start.6
  4.3 0.7 %copy-done.6 = s32[5120]{0:T(1024)S(1)} copy-done((s32[5120]{0:T(1024)S(1)}, s32[5120]{0:T(1024)}, u32[]{:S(2)}) %copy-start.6) | copy-done | bytes 20504
  5.0 0.0 copy-start.7
  5.0 0.7 %copy-done.7 = f32[3,512]{1,0:T(4,128)S(1)} copy-done((f32[3,512]{1,0:T(4,128)S(1)}, f32[3,512]{1,0:T(4,128)}, u32[]{:S(2)}) %copy-start.7) | copy-done | bytes 6168
  5.7 48.2 %shard_map.109 = f32[8,2048]{1,0:T(8,128)S(1)} custom-call(f32[3,2048]{1,0:T(4,128)S(1)} %copy-done.3, f32[8,2048]{1,0:T(8,128)S(1)} %copy-done.2, f32[3,512]{1,0:T(4,128)S(1)} %copy-done.7, f32[3,64]{1,0:T(4,128)S(1)} %copy-done.8, f32[2,64,256]{2,1,0:T(8,128)S(1)} %copy-done, f32[1,64,512]{2,1,0:T(8,128)S(1)} %copy-done.1, s32[5120]{0:T(1024)S(1)} %bitcast.1, ...), custom_call_target="tpu_custom_call" | custom-call | tf_op jit(solution)/shard_map/pallas_call | solution.py:399
  54.0 0.6 %copy.13 = f32[8,2048]{1,0:T(8,128)} copy(f32[8,2048]{1,0:T(8,128)S(1)} %shard_map.109) | data formatting | bytes 131072
Async XLA Ops:
  0.0 0.9 %copy-start.3 = (f32[3,2048]{1,0:T(4,128)S(1)}, f32[3,2048]{1,0:T(4,128)}, u32[]{:S(2)}) copy-start(f32[3,2048]{1,0:T(4,128)} %coords.1) | copy-start | bytes 73732
  0.0 0.9 %copy-start.5 = (s32[5120,1]{0,1:T(1,128)S(1)}, s32[5120,1]{0,1:T(1,128)}, u32[]{:S(2)}) copy-start(s32[5120,1]{0,1:T(1,128)} %param.17) | copy-start | bytes 61444
  0.0 0.9 %copy-start.8 = (f32[3,64]{1,0:T(4,128)S(1)}, f32[3,64]{1,0:T(4,128)}, u32[]{:S(2)}) copy-start(f32[3,64]{1,0:T(4,128)} %parent_skel.1) | copy-start | bytes 2308
  0.0 0.9 %copy-start.9 = (s32[64]{0:T(128)S(1)}, s32[64]{0:T(128)}, u32[]{:S(2)}) copy-start(s32[64]{0:T(128)} %near_count.1) | copy-start | bytes 772
  0.9 0.9 %copy-start = (f32[2,64,256]{2,1,0:T(8,128)S(1)}, f32[2,64,256]{2,1,0:T(8,128)}, u32[]{:S(2)}) copy-start(f32[2,64,256]{2,1,0:T(8,128)} %interp.1) | copy-start | bytes 393220
  1.8 0.9 %copy-start.1 = (f32[1,64,512]{2,1,0:T(8,128)S(1)}, f32[1,64,512]{2,1,0:T(8,128)}, u32[]{:S(2)}) copy-start(f32[1,64,512]{2,1,0:T(8,128)} %transfer.1) | copy-start | bytes 393220
  2.7 0.8 %copy-start.2 = (f32[8,2048]{1,0:T(8,128)S(1)}, f32[8,2048]{1,0:T(8,128)}, u32[]{:S(2)}) copy-start(f32[8,2048]{1,0:T(8,128)} %charges.1) | copy-start | bytes 196612
  3.6 0.7 %copy-start.4 = (s32[6912]{0:T(1024)S(1)}, s32[6912]{0:T(1024)}, u32[]{:S(2)}) copy-start(s32[6912]{0:T(1024)} %far_partner.1) | copy-start | bytes 82948
  4.3 0.7 %copy-start.6 = (s32[5120]{0:T(1024)S(1)}, s32[5120]{0:T(1024)}, u32[]{:S(2)}) copy-start(s32[5120]{0:T(1024)} %near_partner.1) | copy-start | bytes 61444
  5.0 0.7 %copy-start.7 = (f32[3,512]{1,0:T(4,128)S(1)}, f32[3,512]{1,0:T(4,128)}, u32[]{:S(2)}) copy-start(f32[3,512]{1,0:T(4,128)} %leaf_skel.1) | copy-start | bytes 18436
where the time goes:
time: 55 us; the launch traced here: 54.6 us
  Pallas kernels  48.2 us (88%)
  local copies, waits for them, and re-layouts  5.46 us (10%)
  other arithmetic  0.85 us (2%)
    pallas_call x1, Pallas kernels, shards(): pl.pallas_call(functools.partial(kernel, boxes, sides), out_shape=jax.Sha...  48.2 us
    unnamed x21, local copies, waits for them, and re-layouts  5.46 us

commit v1 on v0

v1 whole, which is shorter than its diff:
```python
import functools

import jax
import jax.numpy as jnp
from jax import lax
from jax.experimental import pallas as pl
from jax.experimental.pallas import tpu as pltpu
from jax.sharding import PartitionSpec as P

REACH = 3
SPAN = 2 * REACH + 1
ORDER = (3, 2, 4, 1, 5, 0, 6)
SOFTEN = 0.0025
COUPLE = 0.07957747154594767

LEAF = 256
SKEL = 64
LEAVES = 8
COLS = 8
NEAR_PER = 10
FAR_PER = 12
ENTRIES = 9
NEAR_ROWS = LEAVES * NEAR_PER
FAR_ROWS = ENTRIES * FAR_PER
TABLE = 640

MESH = pl.DeviceIdType.MESH
NN = (((1,), (0,)), ((), ()))
NT = (((1,), (1,)), ((), ()))
f32, bf16, i32 = jnp.float32, jnp.bfloat16, jnp.int32


def split(value):
    high = value.astype(bf16)
    low = (value - high.astype(f32)).astype(bf16)
    return high, low


def stacked(value):
    return jnp.concatenate(split(value), axis=0)


def folded(value):
    return value[:8] + value[8:16]


def mul(a, b, dims=NN):
    return lax.dot_general(a, b, dims, preferred_element_type=f32)


def lane_index(shape):
    return lax.broadcasted_iota(i32, shape, 1)


def row_index(shape):
    return lax.broadcasted_iota(i32, shape, 0)


def column_form(row, width):
    return jnp.transpose(jnp.broadcast_to(row, (128, width)))


def inverse_distance(ax, ay, az, bx, by, bz):
    dx, dy, dz = ax - bx, ay - by, az - bz
    return lax.rsqrt((dx * dx + SOFTEN) + (dy * dy + dz * dz))


def tile_pieces(spread, leaf, points, high, low):
    def piece(c):
        s = pl.ds(c * 32, 32)
        for h in range(2):
            at = slice(h * 128, h * 128 + 128)
            k = inverse_distance(
                spread[0, leaf, s, :], spread[1, leaf, s, :], spread[2, leaf, s, :],
                points[0:1, at], points[1:2, at], points[2:3, at],
            )
            high[s, at], low[s, at] = split(k)

    return [functools.partial(piece, c) for c in range(8)]


def interleave(first, second):
    each = max(1, -(-len(second) // max(1, len(first))))
    for j, step in enumerate(first):
        step()
        for other in second[j * each:(j + 1) * each]:
            other()
    for other in second[len(first) * each:]:
        other()


def kernel(
    boxes, sides,
    coords, charges, leaf_skel, parent_skel, interp, transfer,
    near_offset, near_partner, near_count, far_offset, far_partner,
    out,
    val0, val1, val2, val3, val4, val5, val6,
    pts0, pts1, pts2, pts3, pts4, pts5, pts6,
    charges_v, coords_v, leaf_skel_v, parent_skel_v, transfer_v,
    noff, npart, ncount, foff, fpart, plan_v, plan,
    skel, tables, near_send, near_recv, far_send, far_recv, gathered,
    spread, spread_skel, own_v, kh0, kh1, kl0, kl1, near_run, near_own, own_sum, chosen_far,
    left_t, right_t, k_far, v_far, far_x, far_own, far_mat, ih, il, far_sum,
    s_load, s_plan, s_int, r_int, s_dat, r_dat, s_tab, r_tab, s_near, r_near, s_far, r_far,
):
    me = lax.axis_index("box")
    side = lax.axis_index("rhs")
    others = [o for o in range(SPAN) if o != REACH]
    vals = [val0, val1, val2, val3, val4, val5, val6]
    pts = [pts0, pts1, pts2, pts3, pts4, pts5, pts6]

    def box_at(step):
        return lax.rem(me + (step + boxes), boxes)

    def side_at(step):
        return lax.rem(side + step, sides)

    barrier = pltpu.get_barrier_semaphore()
    for o in others:
        pl.semaphore_signal(barrier, inc=1, device_id={"box": box_at(o - REACH)}, device_id_type=MESH)
    for j in range(1, sides):
        pl.semaphore_signal(barrier, inc=1, device_id={"rhs": side_at(j)}, device_id_type=MESH)

    loads = []
    for src, dst in (
        (charges, charges_v), (coords, coords_v), (leaf_skel, leaf_skel_v), (parent_skel, parent_skel_v),
        (near_offset, noff), (near_partner, npart), (near_count, ncount),
        (far_offset, foff), (far_partner, fpart), (interp, gathered.at[side]), (transfer, transfer_v),
    ):
        copy = pltpu.make_async_copy(src, dst, s_load.at[len(loads)])
        copy.start()
        loads.append(copy)

    for copy in loads[:4]:
        copy.wait()
    for leaf in range(LEAVES):
        at = slice(leaf * LEAF, (leaf + 1) * LEAF)
        vals[0][leaf] = charges_v[:, at]
        pts[0][leaf] = coords_v[:, at]
    skel[REACH, :, :512] = leaf_skel_v[...]
    skel[REACH, :, 512:] = jnp.concatenate([parent_skel_v[...], parent_skel_v[...]], axis=1)

    def remote(src, dst, send, recv, device):
        copy = pltpu.make_async_remote_copy(
            src_ref=src, dst_ref=dst, send_sem=send, recv_sem=recv, device_id=device, device_id_type=MESH
        )
        copy.start()
        return copy

    pl.semaphore_wait(barrier, len(others) + sides - 1)
    interp_copies = [
        remote(interp, gathered.at[side], s_int.at[j - 1], r_int.at[j - 1], {"rhs": side_at(j)})
        for j in range(1, sides)
    ]
    data_copies = [None]
    skel_copies = []
    for g in range(1, SPAN):
        target = {"box": box_at(REACH - ORDER[g])}
        data_copies.append([
            remote(src[0], src[g], s_dat.at[n, g], r_dat.at[n, g], target) for n, src in enumerate((vals, pts))
        ])
    for o in others:
        target = {"box": box_at(REACH - o)}
        skel_copies.append(remote(skel.at[REACH], skel.at[o], s_dat.at[2, o], r_dat.at[2, o], target))

    for leaf in range(LEAVES):
        at = slice(leaf * LEAF, (leaf + 1) * LEAF)
        own_v[leaf] = stacked(charges_v[:, at])
        for d in range(3):
            spread[d, leaf] = column_form(coords_v[d:d + 1, at], LEAF)

    for copy in loads[4:9]:
        copy.wait()
    alive = ncount[me]
    near_base, far_base = me * NEAR_ROWS, me * FAR_ROWS
    lanes = lane_index((1, 128))
    code = jnp.full((1, 128), 63 * 8, i32)
    for k in range(NEAR_ROWS):
        hop = noff[0, near_base + k] - REACH
        group = jnp.where(hop < 0, -2 * hop - 1, 2 * hop)
        one = group * 64 + npart[near_base + k] * 8 + k // NEAR_PER + jnp.where(k < alive, 512, 0)
        code = jnp.where(lanes == k, one, code)
    code_col = column_form(code, 128)
    pair, pair_col = (code >> 3) & 63, (code_col >> 3) & 63
    key, key_col = pair * 128 + lanes, pair_col * 128 + row_index((128, 128))
    rank = jnp.sum((key_col < key).astype(i32), axis=0, keepdims=True)
    placed = column_form(rank, 128) == lanes
    code = jnp.sum(jnp.where(placed, code_col, 0), axis=0, keepdims=True)
    before = pltpu.roll(jnp.broadcast_to(code, (8, 128)), 1, 1)[0:1]
    same = (lanes > 0) & ((code >> 3) & 63 == (before >> 3) & 63)
    upto = jnp.sum((pair_col <= lanes).astype(i32), axis=0, keepdims=True)
    named = jnp.sum((pair_col == lanes).astype(i32), axis=0, keepdims=True)
    plan_v[0:1, :] = code + jnp.where(same, 1024, 0)
    plan_v[1:2, :] = jnp.where(named > 0, upto, 0)
    plan_v[2:3, :] = rank
    plan_v[3:8, :] = jnp.zeros((5, 128), i32)
    plan_copy = pltpu.make_async_copy(plan_v, plan, s_plan)
    plan_copy.start()

    for d in range(3):
        spread_skel[d, :LEAVES * SKEL] = column_form(leaf_skel_v[d:d + 1, :], LEAVES * SKEL)
        spread_skel[d, LEAVES * SKEL:] = column_form(parent_skel_v[d:d + 1, :], SKEL)
    near_run[...] = jnp.zeros_like(near_run)
    pairs = FAR_ROWS // 2
    far_x[pairs * 8:, :] = jnp.zeros((512 - pairs * 8, 128), f32)
    for u in range(2):
        key_row = jnp.full((1, 128), -1, i32)
        for j in range(pairs):
            o, p = foff[0, far_base + 2 * j + u], fpart[far_base + 2 * j + u]
            key = jnp.where(p < LEAVES, o * 8 + p, 8 * SPAN + o)
            key_row = jnp.where((lanes == j) | (lanes == j + 64), key, key_row)
        chosen_far[u * 64:(u + 1) * 64, :] = jnp.where(row_index((64, 128)) == key_row, 1.0, 0.0).astype(bf16)

    buffers = ((kh0, kl0), (kh1, kl1))

    def self_pair(t, carry):
        for u in range(2):
            leaf = t * 2 + u
            for step in tile_pieces(spread, leaf, pts[0][leaf], *buffers[u]):
                step()
        for u in range(2):
            leaf = t * 2 + u
            high, low = buffers[u]
            v = own_v[leaf]
            own_sum[leaf] = folded(mul(v, high[...], NT) + mul(v, low[...], NT))
        return carry

    lax.fori_loop(0, LEAVES // 2, self_pair, 0)

    plan_copy.wait()
    near_copies = []

    def wait_data(g):
        for copy in data_copies[g]:
            copy.wait_recv()

    def near_phase(t, run):
        def rows_of_eight(half, run):
            first = t * 16 + half * 8
            kept_run = [run]

            def pick(bufs, code):
                group, p = (code >> 6) & 7, (code >> 3) & 7
                return jnp.where(
                    group == t, bufs[t][p], jnp.where(group == t + 1, bufs[t + 1][p], bufs[t + 2][p])
                )

            def tile(u):
                code = plan[0, first + u]
                return tile_pieces(spread, code & 7, pick(pts, code), *buffers[u % 2])

            def matmuls(u):
                high, low = buffers[u % 2]
                code = plan[0, first + u]
                kept = {}

                def start():
                    kept["own_v"] = own_v[code & 7]
                    kept["live"] = ((code >> 9) & 1).astype(f32)
                    kept["v"] = stacked(pick(vals, code) * kept["live"])
                    kept["other"] = mul(kept["own_v"], high[...])

                def second():
                    other = folded(kept["other"] + mul(kept["own_v"], low[...]))
                    again = ((code >> 10) & 1).astype(f32)
                    kept_run[0] = kept_run[0] * again + other * kept["live"]
                    near_run[first + u] = kept_run[0]

                def third():
                    kept["own"] = mul(kept["v"], high[...], NT)

                def fourth():
                    near_own[first + u] = folded(kept["own"] + mul(kept["v"], low[...], NT))

                return [start, second, third, fourth]

            for step in tile(0):
                step()
            for u in range(8):
                interleave(matmuls(u), tile(u + 1) if u + 1 < 8 else [])
            return kept_run[0]

        return lax.fori_loop(0, 2, rows_of_eight, run)

    def near_reply(g):
        for p in range(LEAVES):
            last = plan[1, g * 8 + p]
            some = jnp.where(last > 0, 1.0, 0.0).astype(f32)
            near_send[g, p] = near_run[jnp.maximum(last - 1, 0)] * some
        if g:
            near_copies.append(
                remote(near_send.at[g], near_recv.at[g], s_near.at[g], r_near.at[g], {"box": box_at(ORDER[g] - REACH)})
            )

    left = lane_index((8, 128)) < SKEL
    run = jnp.zeros((COLS, LEAF), f32)
    wait_data(1)
    wait_data(2)
    run = near_phase(0, run)
    near_reply(0)

    for copy in loads[9:]:
        copy.wait()
    for copy in interp_copies:
        copy.wait_recv()
    for m in range(4):
        high, low = split(gathered[m].reshape(128, LEAF))
        ih[m], il[m] = high, low
        both = jnp.concatenate([own_v[2 * m], own_v[2 * m + 1]], axis=0)
        got = mul(both, high, NT) + mul(both, low, NT)
        tables[REACH, :, m * 128:(m + 1) * 128] = jnp.where(left, folded(got[:16]), folded(got[16:]))
    t_high, t_low = split(transfer_v[0])
    children = stacked(tables[REACH, :, :LEAVES * SKEL])
    parents = folded(mul(children, t_high, NT) + mul(children, t_low, NT))
    tables[REACH, :, 512:576] = parents
    tables[REACH, :, 576:640] = jnp.zeros((COLS, SKEL), f32)
    table_copies = [
        remote(tables.at[REACH], tables.at[o], s_tab.at[o], r_tab.at[o], {"box": box_at(REACH - o)})
        for o in ORDER[1:]
    ]

    for t in range(1, 5):
        wait_data(t + 2)
        run = near_phase(t, run)
        near_reply(t)
    near_reply(5)
    near_reply(6)

    for copy in skel_copies + table_copies:
        copy.wait_recv()
    left3 = lane_index((3, 128)) < SKEL

    def halves(block, mask):
        turned = pltpu.roll(block, SKEL, 1)
        zero = jnp.zeros_like(block)
        even = (jnp.where(mask, block, zero), jnp.where(mask, zero, turned))
        odd = (jnp.where(mask, turned, zero), jnp.where(mask, zero, block))
        return even, odd

    def put(slot, value_pair, point_pair):
        for table, value, point in zip((left_t, right_t), value_pair, point_pair):
            table[slot, 0:8, :] = value
            table[slot, 8:11, :] = point

    for o in range(SPAN):
        for m in range(4):
            at = slice(m * 128, (m + 1) * 128)
            values = halves(tables[o, :, at], left)
            points = halves(skel[o, :, at], left3)
            for u in range(2):
                put(o * ENTRIES + 2 * m + u, values[u], points[u])
        values = halves(tables[o, :, 512:640], left)
        points = halves(skel[o, :, 512:640], left3)
        put(o * ENTRIES + LEAVES, values[0], points[0])

    def far_slot(k):
        return foff[0, far_base + k] * ENTRIES + fpart[far_base + k]

    def far_entry(e, carry):
        mine = left_t[REACH * ENTRIES + e, 0:8, :] + right_t[REACH * ENTRIES + e, 0:8, :]
        v_own = stacked(mine)
        rows = pl.ds(pl.multiple_of(e * SKEL, SKEL), SKEL)
        for j in range(FAR_PER // 2):
            at = slice(j * 128, (j + 1) * 128)
            k = e * FAR_PER + 2 * j
            block = left_t[far_slot(k), 0:11, :] + right_t[far_slot(k + 1), 0:11, :]
            tile = inverse_distance(
                spread_skel[0, rows, :], spread_skel[1, rows, :], spread_skel[2, rows, :],
                block[8:9], block[9:10], block[10:11],
            )
            k_far[0:SKEL, at], k_far[SKEL:, at] = split(tile)
            v_far[:, at] = stacked(block[0:8])
        tiles = k_far[...]
        other = folded(mul(v_own, tiles))
        for j in range(FAR_PER // 2):
            at = pl.ds(pl.multiple_of((e * (FAR_PER // 2) + j) * 8, 8), 8)
            far_x[at, :] = other[:, j * 128:(j + 1) * 128]
        own = folded(mul(v_far[...], tiles, NT))
        far_own[e] = own + pltpu.roll(own, SKEL, 1)
        return carry

    lax.fori_loop(0, ENTRIES, far_entry, 0)

    for r in range(COLS):
        high, low = split(far_x[pl.ds(r, 64, stride=8), :])
        far_mat[0:64, r * 128:(r + 1) * 128] = high
        far_mat[64:128, r * 128:(r + 1) * 128] = low
    reply = mul(chosen_far[...], far_mat[...])
    left64 = lane_index((64, 128)) < SKEL
    for m in range(4):
        a, b = slice(m * 128, (m + 1) * 128), slice((m + 4) * 128, (m + 5) * 128)
        straight = jnp.where(left64, reply[:64, a], reply[64:, b])
        crossed = jnp.where(left64, reply[:64, b], reply[64:, a])
        whole = straight + pltpu.roll(crossed, SKEL, 1)
        for o in range(SPAN):
            far_send[o, :, a] = whole[8 * o:8 * o + 8]
            far_send[o, m:m + 1, 512:640] = whole[8 * SPAN + o:8 * SPAN + o + 1]
    for o in range(SPAN):
        far_send[o, 4:8, 512:640] = jnp.zeros((4, 128), f32)
    far_copies = [
        remote(far_send.at[o], far_recv.at[o], s_far.at[o], r_far.at[o], {"box": box_at(o - REACH)})
        for o in (0, 6, 1, 5, 2, 4)
    ]

    for leaf in range(LEAVES):
        total = own_sum[leaf] + near_send[0, leaf]
        for u in range(NEAR_PER):
            total = total + near_own[plan[2, leaf * NEAR_PER + u]]
        own_sum[leaf] = total
    for copy in near_copies:
        copy.wait_recv()
    for leaf in range(LEAVES):
        total = own_sum[leaf]
        for g in range(1, SPAN):
            total = total + near_recv[g, leaf]
        own_sum[leaf] = total

    for copy in far_copies:
        copy.wait_recv()
    total = far_send[REACH]
    for o in others:
        total = total + far_recv[o]
    for m in range(4):
        far_sum[m * 8:(m + 1) * 8, :] = total[:, m * 128:(m + 1) * 128]
    fours = total[0:4, 512:640]
    parent = jnp.concatenate([fours, pltpu.roll(fours, SKEL, 1)], axis=0) + far_own[LEAVES]
    parent = stacked(parent[:, :SKEL])
    handed = folded(mul(parent, t_high) + mul(parent, t_low))
    for m in range(4):
        down = handed[:, m * 128:(m + 1) * 128]
        even = far_sum[pl.ds(2 * m, 4, stride=8), :]
        odd = far_sum[pl.ds(2 * m + 1, 4, stride=8), :]
        even = jnp.concatenate([even, pltpu.roll(even, SKEL, 1)], axis=0) + far_own[2 * m] + down
        odd = jnp.concatenate([pltpu.roll(odd, SKEL, 1), odd], axis=0) + far_own[2 * m + 1] + down
        zero = jnp.zeros_like(even)
        both = jnp.concatenate([stacked(jnp.where(left, even, zero)), stacked(jnp.where(left, zero, odd))], axis=0)
        got = mul(both, ih[m]) + mul(both, il[m])
        for u in range(2):
            leaf = 2 * m + u
            out[:, leaf * LEAF:(leaf + 1) * LEAF] = COUPLE * (own_sum[leaf] + folded(got[16 * u:16 * u + 16]))

    for copy in interp_copies + sum(data_copies[1:], []) + skel_copies + table_copies + near_copies + far_copies:
        copy.wait_send()


def shards(
    leaf_coords, charges, leaf_skeleton, parent_skeleton, interp, transfer,
    near_offset, near_partner, near_count, far_offset, far_partner,
):
    boxes, sides = lax.axis_size("box"), lax.axis_size("rhs")
    V, S, M = pltpu.VMEM, pltpu.SemaphoreType.DMA, pltpu.SMEM
    operands = (
        leaf_coords, charges, leaf_skeleton, parent_skeleton, interp, transfer,
        near_offset.reshape(1, -1), near_partner, near_count, far_offset.reshape(1, -1), far_partner,
    )
    return pl.pallas_call(
        functools.partial(kernel, boxes, sides),
        out_shape=jax.ShapeDtypeStruct(charges.shape, f32),
        in_specs=[pl.BlockSpec(memory_space=pltpu.HBM)] * len(operands),
        out_specs=pl.BlockSpec(memory_space=pltpu.VMEM),
        scratch_shapes=[V((LEAVES, COLS, LEAF), f32)] * SPAN
        + [V((LEAVES, 3, LEAF), f32)] * SPAN
        + [V(a.shape, f32) for a in (charges, leaf_coords, leaf_skeleton, parent_skeleton, transfer)]
        + [M(a.shape, i32) for a in operands[6:]]
        + [
            V((8, 128), i32),
            M((8, 128), i32),
            V((SPAN, 3, TABLE), f32),
            V((SPAN, COLS, TABLE), f32),
            V((SPAN, LEAVES, COLS, LEAF), f32),
            V((SPAN, LEAVES, COLS, LEAF), f32),
            V((SPAN, 8, TABLE), f32),
            V((SPAN, 8, TABLE), f32),
            V((4, 2, SKEL, LEAF), f32),
            V((3, LEAVES, LEAF, 128), f32),
            V((3, ENTRIES * SKEL, 128), f32),
            V((LEAVES, 16, LEAF), bf16),
            V((LEAF, LEAF), bf16),
            V((LEAF, LEAF), bf16),
            V((LEAF, LEAF), bf16),
            V((LEAF, LEAF), bf16),
            V((NEAR_ROWS, COLS, LEAF), f32),
            V((NEAR_ROWS, COLS, LEAF), f32),
            V((LEAVES, COLS, LEAF), f32),
            V((128, 128), bf16),
            V((64, 16, 128), f32),
            V((64, 16, 128), f32),
            V((128, FAR_PER * SKEL), bf16),
            V((16, FAR_PER * SKEL), bf16),
            V((512, 128), f32),
            V((ENTRIES, 8, 128), f32),
            V((128, 1024), bf16),
            V((4, 128, LEAF), bf16),
            V((4, 128, LEAF), bf16),
            V((32, 128), f32),
            S((11,)), S(()), S((3,)), S((3,)), S((3, SPAN)), S((3, SPAN)), S((SPAN,)), S((SPAN,)),
            S((SPAN,)), S((SPAN,)), S((SPAN,)), S((SPAN,)),
        ],
        compiler_params=pltpu.CompilerParams(
            collective_id=0, has_side_effects=True, vmem_limit_bytes=60 * 2**20
        ),
    )(*operands)


def solution(mesh):
    return jax.shard_map(
        shards,
        mesh=mesh,
        in_specs=(
            P(None, "box"),
            P("rhs", "box"),
            P(None, "box"),
            P(None, "box"),
            P(("box", "rhs"), None, None),
            P("box", None, None),
            P(),
            P(),
            P(),
            P(),
            P(),
        ),
        out_specs=P("rhs", "box"),
        check_vma=False,
    )
```

time: 55 us -> 45.7 us (0.83)
  Pallas kernels: 48.2 us -> 44.1 us
  local copies, waits for them, and re-layouts: 5.46 us -> 1.47 us
  other arithmetic: 0.85 us -> 0 us
    pallas_call x1, Pallas kernels: 48.2 us -> 44.1 us  [shards(): pl.pallas_call(functools.partial(kernel, boxes, sides), out_shape=jax.Sha...]
    unnamed x21 -> x1, local copies, waits for them, and re-layouts: 5.46 us -> 1.47 us
    unnamed x1 -> x0, other arithmetic: 0.85 us -> none
where the time goes in v1:
time: 45.7 us; the launch traced here: 45.5 us
  Pallas kernels  44.1 us (96%)
  local copies, waits for them, and re-layouts  1.47 us (3%)
    pallas_call x1, Pallas kernels, shards(): pl.pallas_call(functools.partial(kernel, boxes, sides), out_shape=jax.Sha...  44.1 us
    unnamed x1, local copies, waits for them, and re-layouts  1.47 us

profile of v1, /device:TPU:1, one launch (start us, length us, event | category | flops | bytes accessed | tf_op | source)
XLA Modules:
  0.0 45.5 jit_solution(17772299674224849269)
XLA Ops:
  0.0 44.1 %shard_map.109 = f32[8,2048]{1,0:T(8,128)} custom-call(f32[3,2048]{1,0:T(4,128)} %coords.1, f32[8,2048]{1,0:T(8,128)} %charges.1, f32[3,512]{1,0:T(4,128)} %leaf_skel.1, f32[3,64]{1,0:T(4,128)} %parent_skel.1, f32[2,64,256]{2,1,0:T(8,128)} %interp.1, f32[1,64,512]{2,1,0:T(8,128)} %transfer.1, s32[1,5120]{1,0:T(1,128)} %bitcast.3, s32[5120]{0:T(1024)} %near_partner.1, ...), custom_call_target="tpu_custom_call" | custom-call | tf_op jit(solution)/shard_map/pallas_call | solution.py:456
  44.1 1.5 %copy.13 = f32[8,2048]{1,0:T(8,128)} copy(f32[8,2048]{1,0:T(8,128)} %shard_map.109) | data formatting | bytes 131072

commit v2 on v1

v2 whole, which is shorter than its diff:
```python
import functools

import jax
import jax.numpy as jnp
from jax import lax
from jax.experimental import pallas as pl
from jax.experimental.pallas import tpu as pltpu
from jax.sharding import PartitionSpec as P

REACH = 3
SPAN = 2 * REACH + 1
ORDER = (4, 5, 6, 3, 2, 1, 0)
HOME = 3
AWAY = (0, 1, 2, 4, 5, 6)
SOFTEN = 0.0025
COUPLE = 0.07957747154594767

LEAF = 256
SKEL = 64
LEAVES = 8
COLS = 8
NEAR_PER = 10
FAR_PER = 12
ENTRIES = 9
NEAR_ROWS = LEAVES * NEAR_PER
FAR_ROWS = ENTRIES * FAR_PER
TABLE = 640

MESH = pl.DeviceIdType.MESH
NN = (((1,), (0,)), ((), ()))
NT = (((1,), (1,)), ((), ()))
f32, bf16, i32 = jnp.float32, jnp.bfloat16, jnp.int32


def split(value):
    high = value.astype(bf16)
    low = (value - high.astype(f32)).astype(bf16)
    return high, low


def stacked(value):
    return jnp.concatenate(split(value), axis=0)


def folded(value):
    return value[:8] + value[8:16]


def mul(a, b, dims=NN):
    return lax.dot_general(a, b, dims, preferred_element_type=f32)


def lane_index(shape):
    return lax.broadcasted_iota(i32, shape, 1)


def row_index(shape):
    return lax.broadcasted_iota(i32, shape, 0)


def column_form(row, width):
    return jnp.transpose(jnp.broadcast_to(row, (128, width)))


def inverse_distance(ax, ay, az, bx, by, bz):
    dx, dy, dz = ax - bx, ay - by, az - bz
    return lax.rsqrt((dx * dx + SOFTEN) + (dy * dy + dz * dz))


def tile_pieces(spread, leaf, points, high, low):
    def piece(c):
        s = pl.ds(c * 32, 32)
        for h in range(2):
            at = slice(h * 128, h * 128 + 128)
            k = inverse_distance(
                spread[0, leaf, s, :], spread[1, leaf, s, :], spread[2, leaf, s, :],
                points[0:1, at], points[1:2, at], points[2:3, at],
            )
            high[s, at], low[s, at] = split(k)

    return [functools.partial(piece, c) for c in range(8)]


def interleave(first, second):
    each = max(1, -(-len(second) // max(1, len(first))))
    for j, step in enumerate(first):
        step()
        for other in second[j * each:(j + 1) * each]:
            other()
    for other in second[len(first) * each:]:
        other()


def kernel(
    boxes, sides,
    coords, charges, leaf_skel, parent_skel, interp, transfer,
    near_offset, near_partner, near_count, far_offset, far_partner,
    out,
    vals_in, pts_in, vals, pts, mixed, parts, part_send, th, tl,
    charges_v, coords_v, leaf_skel_v, parent_skel_v, transfer_v,
    noff, npart, ncount, foff, fpart, plan_v, plan,
    skel, tables, near_send, near_recv, far_send, far_recv, gathered,
    spread, spread_skel, own_v, kh0, kh1, kl0, kl1, near_run, near_own, own_sum, chosen_far,
    left_t, right_t, k_far, v_far, far_x, far_own, far_mat, ih, il, far_sum,
    s_load, s_plan, s_mix, r_mix, s_part, r_part, s_int, r_int, s_dat, r_dat, s_tab, r_tab, s_near, r_near, s_far, r_far,
):
    me = lax.axis_index("box")
    side = lax.axis_index("rhs")
    others = [o for o in range(SPAN) if o != REACH]

    def box_at(step):
        return lax.rem(me + (step + boxes), boxes)

    def side_at(step):
        return lax.rem(side + step, sides)

    barrier = pltpu.get_barrier_semaphore()
    for o in others:
        pl.semaphore_signal(barrier, inc=1, device_id={"box": box_at(o - REACH)}, device_id_type=MESH)
    for j in range(1, sides):
        pl.semaphore_signal(barrier, inc=1, device_id={"rhs": side_at(j)}, device_id_type=MESH)

    loads = []
    for src, dst in (
        (charges, charges_v), (coords, coords_v), (leaf_skel, leaf_skel_v), (parent_skel, parent_skel_v),
        (near_offset, noff), (near_partner, npart), (near_count, ncount),
        (far_offset, foff), (far_partner, fpart), (interp, gathered.at[side]), (transfer, transfer_v),
    ):
        copy = pltpu.make_async_copy(src, dst, s_load.at[len(loads)])
        copy.start()
        loads.append(copy)

    for copy in loads[:4]:
        copy.wait()
    for leaf in range(LEAVES):
        at = slice(leaf * LEAF, (leaf + 1) * LEAF)
        vals_in[HOME, leaf] = charges_v[:, at]
        pts_in[HOME, leaf] = coords_v[:, at]
        vals[HOME * LEAVES + leaf] = charges_v[:, at]
        pts[HOME * LEAVES + leaf] = coords_v[:, at]
    skel[REACH, :, :512] = leaf_skel_v[...]
    skel[REACH, :, 512:] = jnp.concatenate([parent_skel_v[...], parent_skel_v[...]], axis=1)

    def remote(src, dst, send, recv, device):
        copy = pltpu.make_async_remote_copy(
            src_ref=src, dst_ref=dst, send_sem=send, recv_sem=recv, device_id=device, device_id_type=MESH
        )
        copy.start()
        return copy

    pl.semaphore_wait(barrier, len(others) + sides - 1)
    two = 2 * LEAF
    mix_copies = [
        remote(
            charges_v.at[:, pl.ds(pl.multiple_of(side_at(j) * two, two), two)], mixed.at[side],
            s_mix.at[j - 1], r_mix.at[j - 1], {"rhs": side_at(j)},
        )
        for j in range(1, sides)
    ]

    def data_copy(n, g, target):
        src = (vals_in, pts_in)[n]
        return pltpu.make_async_remote_copy(
            src_ref=src.at[HOME], dst_ref=src.at[g], send_sem=s_dat.at[n, g], recv_sem=r_dat.at[n, g],
            device_id=target, device_id_type=MESH,
        )

    data_copies, skel_copies = [], []
    for g in AWAY:
        target = {"box": box_at(REACH - ORDER[g])}
        for n in range(2):
            copy = data_copy(n, g, target)
            copy.start()
            data_copies.append(copy)
    for o in others:
        target = {"box": box_at(REACH - o)}
        skel_copies.append(remote(skel.at[REACH], skel.at[o], s_dat.at[2, o], r_dat.at[2, o], target))

    for leaf in range(LEAVES):
        at = slice(leaf * LEAF, (leaf + 1) * LEAF)
        own_v[leaf] = stacked(charges_v[:, at])
        for d in range(3):
            spread[d, leaf] = column_form(coords_v[d:d + 1, at], LEAF)

    for copy in loads[4:9]:
        copy.wait()
    alive = ncount[me]
    near_base, far_base = me * NEAR_ROWS, me * FAR_ROWS
    lanes = lane_index((1, 128))
    code = jnp.full((1, 128), 63 * 8, i32)
    for k in range(NEAR_ROWS):
        hop = noff[0, near_base + k] - REACH
        group = jnp.where(hop > 0, hop - 1, HOME - hop)
        one = group * 64 + npart[near_base + k] * 8 + k // NEAR_PER + jnp.where(k < alive, 512, 0)
        code = jnp.where(lanes == k, one, code)
    code_col = column_form(code, 128)
    pair, pair_col = (code >> 3) & 63, (code_col >> 3) & 63
    key, key_col = pair * 128 + lanes, pair_col * 128 + row_index((128, 128))
    rank = jnp.sum((key_col < key).astype(i32), axis=0, keepdims=True)
    placed = column_form(rank, 128) == lanes
    code = jnp.sum(jnp.where(placed, code_col, 0), axis=0, keepdims=True)
    before = pltpu.roll(jnp.broadcast_to(code, (8, 128)), 1, 1)[0:1]
    same = (lanes > 0) & ((code >> 3) & 63 == (before >> 3) & 63)
    upto = jnp.sum((pair_col <= lanes).astype(i32), axis=0, keepdims=True)
    named = jnp.sum((pair_col == lanes).astype(i32), axis=0, keepdims=True)
    plan_v[0:1, :] = code + jnp.where(same, 1024, 0)
    plan_v[1:2, :] = jnp.where(named > 0, upto, 0)
    plan_v[2:3, :] = rank
    plan_v[3:8, :] = jnp.zeros((5, 128), i32)
    plan_copy = pltpu.make_async_copy(plan_v, plan, s_plan)
    plan_copy.start()

    for d in range(3):
        spread_skel[d, :LEAVES * SKEL] = column_form(leaf_skel_v[d:d + 1, :], LEAVES * SKEL)
        spread_skel[d, LEAVES * SKEL:] = column_form(parent_skel_v[d:d + 1, :], SKEL)
    near_run[...] = jnp.zeros_like(near_run)
    pairs = FAR_ROWS // 2
    far_x[pairs * 8:, :] = jnp.zeros((512 - pairs * 8, 128), f32)
    for u in range(2):
        key_row = jnp.full((1, 128), -1, i32)
        for j in range(pairs):
            o, p = foff[0, far_base + 2 * j + u], fpart[far_base + 2 * j + u]
            key = jnp.where(p < LEAVES, o * 8 + p, 8 * SPAN + o)
            key_row = jnp.where((lanes == j) | (lanes == j + 64), key, key_row)
        chosen_far[u * 64:(u + 1) * 64, :] = jnp.where(row_index((64, 128)) == key_row, 1.0, 0.0).astype(bf16)

    buffers = ((kh0, kl0), (kh1, kl1))

    def self_pair(t, carry):
        for u in range(2):
            leaf = t * 2 + u
            for step in tile_pieces(spread, leaf, pts[HOME * LEAVES + leaf], *buffers[u]):
                step()
        for u in range(2):
            leaf = t * 2 + u
            high, low = buffers[u]
            v = own_v[leaf]
            own_sum[leaf] = folded(mul(v, high[...], NT) + mul(v, low[...], NT))
        return carry

    lax.fori_loop(0, LEAVES // 2, self_pair, 0)

    left = lane_index((8, 128)) < SKEL
    for copy in loads[9:]:
        copy.wait()
    mixed[side] = charges_v[:, pl.ds(pl.multiple_of(side * two, two), two)]
    for copy in mix_copies:
        copy.wait_recv()
    high, low = split(gathered[side].reshape(128, LEAF))
    columns = [
        jnp.concatenate([mixed[q, :, u * LEAF:(u + 1) * LEAF] for q in range(4)], axis=0) for u in range(2)
    ]
    both = jnp.concatenate([stacked(columns[0]), stacked(columns[1])], axis=0)
    got = mul(both, high, NT) + mul(both, low, NT)
    weights = jnp.where(
        lane_index((32, 128)) < SKEL, got[0:32] + got[32:64], got[64:96] + got[96:128]
    )
    high, low = split(transfer_v[0, :, pl.ds(pl.multiple_of(side * 128, 128), 128)])
    both = stacked(weights)
    got = mul(both, high, NT) + mul(both, low, NT)
    got = got[:32] + got[32:]
    part_send[:, 0:128] = weights
    part_send[:, 128:256] = jnp.concatenate([got, got], axis=1)
    part_copies = [
        remote(
            part_send.at[pl.ds(pl.multiple_of(side_at(j) * 8, 8), 8)], parts.at[side],
            s_part.at[j - 1], r_part.at[j - 1], {"rhs": side_at(j)},
        )
        for j in range(1, sides)
    ]
    parts[side] = part_send[pl.ds(pl.multiple_of(side * 8, 8), 8), :]
    th[...], tl[...] = split(transfer_v[0])

    plan_copy.wait()

    def arrive(g):
        here = {"box": box_at(1)}
        for n in range(2):
            data_copy(n, g, here).wait_recv()
        for leaf in range(LEAVES):
            vals[g * LEAVES + leaf] = vals_in[g, leaf]
            pts[g * LEAVES + leaf] = pts_in[g, leaf]

    def table_copy(g, step):
        slot = step + REACH
        return pltpu.make_async_remote_copy(
            src_ref=tables.at[REACH], dst_ref=tables.at[slot], send_sem=s_tab.at[slot], recv_sem=r_tab.at[slot],
            device_id={"box": box_at(-step)}, device_id_type=MESH,
        )

    def reply_copy(g, step):
        return pltpu.make_async_remote_copy(
            src_ref=near_send.at[g], dst_ref=near_recv.at[g], send_sem=s_near.at[g], recv_sem=r_near.at[g],
            device_id={"box": box_at(step)}, device_id_type=MESH,
        )

    def interp_copy(j):
        return pltpu.make_async_remote_copy(
            src_ref=interp, dst_ref=gathered.at[side], send_sem=s_int.at[j - 1], recv_sem=r_int.at[j - 1],
            device_id={"rhs": side_at(j)}, device_id_type=MESH,
        )

    def far_copy(o):
        return pltpu.make_async_remote_copy(
            src_ref=far_send.at[o], dst_ref=far_recv.at[o], send_sem=s_far.at[o], recv_sem=r_far.at[o],
            device_id={"box": box_at(o - REACH)}, device_id_type=MESH,
        )

    def near_reply(g):
        for p in range(LEAVES):
            last = plan[1, g * 8 + p]
            some = jnp.where(last > 0, 1.0, 0.0).astype(f32)
            near_send[g, p] = near_run[jnp.maximum(last - 1, 0)] * some

    def near_phase(t, run):
        @pl.when(t > 1)
        def _():
            arrive(t + 2)

        first = t * 16
        kept_run = [run]

        def tile(u):
            code = plan[0, first + u]
            return tile_pieces(spread, code & 7, pts[(code >> 3) & 63], *buffers[u % 2])

        def matmuls(u):
            high, low = buffers[u % 2]
            code = plan[0, first + u]
            kept = {}

            def start():
                kept["live"] = ((code >> 9) & 1).astype(f32)
                kept["v"] = stacked(vals[(code >> 3) & 63] * kept["live"])
                kept["own"] = mul(kept["v"], high[...], NT)

            def second():
                near_own[first + u] = folded(kept["own"] + mul(kept["v"], low[...], NT))

            def third():
                kept["own_v"] = own_v[code & 7]
                kept["other"] = mul(kept["own_v"], high[...])

            def fourth():
                other = folded(kept["other"] + mul(kept["own_v"], low[...]))
                again = ((code >> 10) & 1).astype(f32)
                kept_run[0] = kept_run[0] * again + other * kept["live"]
                near_run[first + u] = kept_run[0]

            return [start, second, third, fourth]

        for step in tile(0):
            step()
        for u in range(16):
            interleave(matmuls(u), tile(u + 1) if u + 1 < 16 else [])

        @pl.when(t < 3)
        def _():
            near_reply(t)
            reply_copy(t, t + 1).start()

        @pl.when(t == 0)
        def _():
            send_table()

        @pl.when(t == 2)
        def _():
            far_pairs()

        return kept_run[0]

    def send_table():
        for copy in part_copies:
            copy.wait_recv()
        total = parts[0, :, 128:256]
        for m in range(4):
            tables[REACH, :, m * 128:(m + 1) * 128] = parts[m, :, 0:128]
            if m:
                total = total + parts[m, :, 128:256]
        tables[REACH, :, 512:640] = total
        for g in AWAY:
            table_copy(g, ORDER[g] - REACH).start()
        for j in range(1, sides):
            interp_copy(j).start()

    def far_pairs():
        for copy in skel_copies:
            copy.wait_recv()
        for o in others:
            table_copy(0, o - REACH).wait_recv()
        left3 = lane_index((3, 128)) < SKEL

        def halves(block, mask):
            turned = pltpu.roll(block, SKEL, 1)
            zero = jnp.zeros_like(block)
            even = (jnp.where(mask, block, zero), jnp.where(mask, zero, turned))
            odd = (jnp.where(mask, turned, zero), jnp.where(mask, zero, block))
            return even, odd

        def put(slot, value_pair, point_pair):
            for table, value, point in zip((left_t, right_t), value_pair, point_pair):
                table[slot, 0:8, :] = value
                table[slot, 8:11, :] = point

        for o in range(SPAN):
            for m in range(4):
                at = slice(m * 128, (m + 1) * 128)
                values = halves(tables[o, :, at], left)
                points = halves(skel[o, :, at], left3)
                for u in range(2):
                    put(o * ENTRIES + 2 * m + u, values[u], points[u])
            values = halves(tables[o, :, 512:640], left)
            points = halves(skel[o, :, 512:640], left3)
            put(o * ENTRIES + LEAVES, values[0], points[0])

        def far_slot(k):
            return foff[0, far_base + k] * ENTRIES + fpart[far_base + k]

        def far_three(t, carry):
            def tiles(u):
                e = t * 3 + u
                rows = pl.ds(pl.multiple_of(e * SKEL, SKEL), SKEL)
                for j in range(FAR_PER // 2):
                    at = slice(j * 128, (j + 1) * 128)
                    k = e * FAR_PER + 2 * j
                    block = left_t[far_slot(k), 0:11, :] + right_t[far_slot(k + 1), 0:11, :]
                    tile = inverse_distance(
                        spread_skel[0, rows, :], spread_skel[1, rows, :], spread_skel[2, rows, :],
                        block[8:9], block[9:10], block[10:11],
                    )
                    k_far[u, 0:SKEL, at], k_far[u, SKEL:, at] = split(tile)
                    v_far[u, :, at] = stacked(block[0:8])

            def matmuls(u):
                e = t * 3 + u
                mine = left_t[REACH * ENTRIES + e, 0:8, :] + right_t[REACH * ENTRIES + e, 0:8, :]
                every = k_far[u]
                other = folded(mul(stacked(mine), every))
                for j in range(FAR_PER // 2):
                    at = pl.ds(pl.multiple_of((e * (FAR_PER // 2) + j) * 8, 8), 8)
                    far_x[at, :] = other[:, j * 128:(j + 1) * 128]
                own = folded(mul(v_far[u], every, NT))
                far_own[e] = own + pltpu.roll(own, SKEL, 1)

            tiles(0)
            tiles(1)
            matmuls(0)
            tiles(2)
            matmuls(1)
            matmuls(2)
            return carry

        lax.fori_loop(0, ENTRIES // 3, far_three, 0)

        for r in range(COLS):
            high, low = split(far_x[pl.ds(r, 64, stride=8), :])
            far_mat[0:64, r * 128:(r + 1) * 128] = high
            far_mat[64:128, r * 128:(r + 1) * 128] = low
        reply = mul(chosen_far[...], far_mat[...])
        left64 = lane_index((64, 128)) < SKEL
        for m in range(4):
            a, b = slice(m * 128, (m + 1) * 128), slice((m + 4) * 128, (m + 5) * 128)
            straight = jnp.where(left64, reply[:64, a], reply[64:, b])
            crossed = jnp.where(left64, reply[:64, b], reply[64:, a])
            whole = straight + pltpu.roll(crossed, SKEL, 1)
            for o in range(SPAN):
                far_send[o, :, a] = whole[8 * o:8 * o + 8]
                far_send[o, m:m + 1, 512:640] = whole[8 * SPAN + o:8 * SPAN + o + 1]
        for o in range(SPAN):
            far_send[o, 4:8, 512:640] = jnp.zeros((4, 128), f32)
        for o in (4, 5, 6, 2, 1, 0):
            far_copy(o).start()

    for g in range(3):
        arrive(g)
    lax.fori_loop(0, 5, near_phase, jnp.zeros((COLS, LEAF), f32))
    for g in (4, 5, 6):
        near_reply(g)
        reply_copy(g, ORDER[g] - REACH).start()
    near_reply(HOME)

    for leaf in range(LEAVES):
        total = own_sum[leaf] + near_send[HOME, leaf]
        for u in range(NEAR_PER):
            total = total + near_own[plan[2, leaf * NEAR_PER + u]]
        own_sum[leaf] = total
    for g in AWAY:
        reply_copy(g, 1).wait_recv()
    for leaf in range(LEAVES):
        total = own_sum[leaf]
        for g in AWAY:
            total = total + near_recv[g, leaf]
        own_sum[leaf] = total

    for j in range(1, sides):
        interp_copy(j).wait_recv()
    for m in range(4):
        ih[m], il[m] = split(gathered[m].reshape(128, LEAF))
    for o in others:
        far_copy(o).wait_recv()
    total = far_send[REACH]
    for o in others:
        total = total + far_recv[o]
    for m in range(4):
        far_sum[m * 8:(m + 1) * 8, :] = total[:, m * 128:(m + 1) * 128]
    fours = total[0:4, 512:640]
    parent = jnp.concatenate([fours, pltpu.roll(fours, SKEL, 1)], axis=0) + far_own[LEAVES]
    parent = stacked(parent[:, :SKEL])
    handed = folded(mul(parent, th[...]) + mul(parent, tl[...]))
    for m in range(4):
        down = handed[:, m * 128:(m + 1) * 128]
        even = far_sum[pl.ds(2 * m, 4, stride=8), :]
        odd = far_sum[pl.ds(2 * m + 1, 4, stride=8), :]
        even = jnp.concatenate([even, pltpu.roll(even, SKEL, 1)], axis=0) + far_own[2 * m] + down
        odd = jnp.concatenate([pltpu.roll(odd, SKEL, 1), odd], axis=0) + far_own[2 * m + 1] + down
        zero = jnp.zeros_like(even)
        both = jnp.concatenate([stacked(jnp.where(left, even, zero)), stacked(jnp.where(left, zero, odd))], axis=0)
        got = mul(both, ih[m]) + mul(both, il[m])
        for u in range(2):
            leaf = 2 * m + u
            out[:, leaf * LEAF:(leaf + 1) * LEAF] = COUPLE * (own_sum[leaf] + folded(got[16 * u:16 * u + 16]))

    for copy in mix_copies + data_copies + skel_copies + part_copies:
        copy.wait_send()
    for j in range(1, sides):
        interp_copy(j).wait_send()
    for g in AWAY:
        step = ORDER[g] - REACH
        table_copy(g, step).wait_send()
        reply_copy(g, step).wait_send()
        far_copy(ORDER[g]).wait_send()


def shards(
    leaf_coords, charges, leaf_skeleton, parent_skeleton, interp, transfer,
    near_offset, near_partner, near_count, far_offset, far_partner,
):
    boxes, sides = lax.axis_size("box"), lax.axis_size("rhs")
    V, S, M = pltpu.VMEM, pltpu.SemaphoreType.DMA, pltpu.SMEM
    operands = (
        leaf_coords, charges, leaf_skeleton, parent_skeleton, interp, transfer,
        near_offset.reshape(1, -1), near_partner, near_count, far_offset.reshape(1, -1), far_partner,
    )
    return pl.pallas_call(
        functools.partial(kernel, boxes, sides),
        out_shape=jax.ShapeDtypeStruct(charges.shape, f32),
        in_specs=[pl.BlockSpec(memory_space=pltpu.HBM)] * len(operands),
        out_specs=pl.BlockSpec(memory_space=pltpu.VMEM),
        scratch_shapes=[
            V((SPAN, LEAVES, COLS, LEAF), f32),
            V((SPAN, LEAVES, 3, LEAF), f32),
            V((SPAN * LEAVES, COLS, LEAF), f32),
            V((SPAN * LEAVES, 3, LEAF), f32),
            V((4, COLS, 2 * LEAF), f32),
            V((4, COLS, 256), f32),
            V((32, 256), f32),
            V((SKEL, 512), bf16),
            V((SKEL, 512), bf16),
        ]
        + [V(a.shape, f32) for a in (charges, leaf_coords, leaf_skeleton, parent_skeleton, transfer)]
        + [M(a.shape, i32) for a in operands[6:]]
        + [
            V((8, 128), i32),
            M((8, 128), i32),
            V((SPAN, 3, TABLE), f32),
            V((SPAN, COLS, TABLE), f32),
            V((SPAN, LEAVES, COLS, LEAF), f32),
            V((SPAN, LEAVES, COLS, LEAF), f32),
            V((SPAN, 8, TABLE), f32),
            V((SPAN, 8, TABLE), f32),
            V((4, 2, SKEL, LEAF), f32),
            V((3, LEAVES, LEAF, 128), f32),
            V((3, ENTRIES * SKEL, 128), f32),
            V((LEAVES, 16, LEAF), bf16),
            V((LEAF, LEAF), bf16),
            V((LEAF, LEAF), bf16),
            V((LEAF, LEAF), bf16),
            V((LEAF, LEAF), bf16),
            V((NEAR_ROWS, COLS, LEAF), f32),
            V((NEAR_ROWS, COLS, LEAF), f32),
            V((LEAVES, COLS, LEAF), f32),
            V((128, 128), bf16),
            V((64, 16, 128), f32),
            V((64, 16, 128), f32),
            V((3, 128, FAR_PER * SKEL), bf16),
            V((3, 16, FAR_PER * SKEL), bf16),
            V((512, 128), f32),
            V((ENTRIES, 8, 128), f32),
            V((128, 1024), bf16),
            V((4, 128, LEAF), bf16),
            V((4, 128, LEAF), bf16),
            V((32, 128), f32),
            S((11,)), S(()), S((3,)), S((3,)), S((3,)), S((3,)), S((3,)), S((3,)), S((3, SPAN)), S((3, SPAN)), S((SPAN,)), S((SPAN,)),
            S((SPAN,)), S((SPAN,)), S((SPAN,)), S((SPAN,)),
        ],
        compiler_params=pltpu.CompilerParams(
            collective_id=0, has_side_effects=True, vmem_limit_bytes=60 * 2**20
        ),
    )(*operands)


def solution(mesh):
    return jax.shard_map(
        shards,
        mesh=mesh,
        in_specs=(
            P(None, "box"),
            P("rhs", "box"),
            P(None, "box"),
            P(None, "box"),
            P(("box", "rhs"), None, None),
            P("box", None, None),
            P(),
            P(),
            P(),
            P(),
            P(),
        ),
        out_specs=P("rhs", "box"),
        check_vma=False,
    )
```

time: 45.7 us -> 41.5 us (0.908)
  Pallas kernels: 44.1 us -> 39.6 us
    pallas_call x1, Pallas kernels: 44.1 us -> 39.6 us  [shards(): pl.pallas_call(functools.partial(kernel, boxes, sides), out_shape=jax.Sha...]
where the time goes in v2:
time: 41.5 us; the launch traced here: 41.1 us
  Pallas kernels  39.6 us (95%)
  local copies, waits for them, and re-layouts  1.47 us (4%)
    pallas_call x1, Pallas kernels, shards(): pl.pallas_call(functools.partial(kernel, boxes, sides), out_shape=jax.Sha...  39.6 us
    unnamed x1, local copies, waits for them, and re-layouts  1.47 us

profile of v2, /device:TPU:1, one launch (start us, length us, event | category | flops | bytes accessed | tf_op | source)
XLA Modules:
  0.0 41.1 jit_solution(13826917671510253561)
XLA Ops:
  0.0 39.6 %shard_map.109 = f32[8,2048]{1,0:T(8,128)} custom-call(f32[3,2048]{1,0:T(4,128)} %coords.1, f32[8,2048]{1,0:T(8,128)} %charges.1, f32[3,512]{1,0:T(4,128)} %leaf_skel.1, f32[3,64]{1,0:T(4,128)} %parent_skel.1, f32[2,64,256]{2,1,0:T(8,128)} %interp.1, f32[1,64,512]{2,1,0:T(8,128)} %transfer.1, s32[1,5120]{1,0:T(1,128)} %bitcast.3, s32[5120]{0:T(1024)} %near_partner.1, ...), custom_call_target="tpu_custom_call" | custom-call | tf_op jit(solution)/shard_map/pallas_call | solution.py:544
  39.6 1.5 %copy.13 = f32[8,2048]{1,0:T(8,128)} copy(f32[8,2048]{1,0:T(8,128)} %shard_map.109) | data formatting | bytes 131072

commit v3 on v2

--- a/solution.py
+++ b/solution.py
@@ -210,36 +210,6 @@
     plan_copy = pltpu.make_async_copy(plan_v, plan, s_plan)
     plan_copy.start()
 
-    for d in range(3):
-        spread_skel[d, :LEAVES * SKEL] = column_form(leaf_skel_v[d:d + 1, :], LEAVES * SKEL)
-        spread_skel[d, LEAVES * SKEL:] = column_form(parent_skel_v[d:d + 1, :], SKEL)
-    near_run[...] = jnp.zeros_like(near_run)
-    pairs = FAR_ROWS // 2
-    far_x[pairs * 8:, :] = jnp.zeros((512 - pairs * 8, 128), f32)
-    for u in range(2):
-        key_row = jnp.full((1, 128), -1, i32)
-        for j in range(pairs):
-            o, p = foff[0, far_base + 2 * j + u], fpart[far_base + 2 * j + u]
-            key = jnp.where(p < LEAVES, o * 8 + p, 8 * SPAN + o)
-            key_row = jnp.where((lanes == j) | (lanes == j + 64), key, key_row)
-        chosen_far[u * 64:(u + 1) * 64, :] = jnp.where(row_index((64, 128)) == key_row, 1.0, 0.0).astype(bf16)
-
-    buffers = ((kh0, kl0), (kh1, kl1))
-
-    def self_pair(t, carry):
-        for u in range(2):
-            leaf = t * 2 + u
-            for step in tile_pieces(spread, leaf, pts[HOME * LEAVES + leaf], *buffers[u]):
-                step()
-        for u in range(2):
-            leaf = t * 2 + u
-            high, low = buffers[u]
-            v = own_v[leaf]
-            own_sum[leaf] = folded(mul(v, high[...], NT) + mul(v, low[...], NT))
-        return carry
-
-    lax.fori_loop(0, LEAVES // 2, self_pair, 0)
-
     left = lane_index((8, 128)) < SKEL
     for copy in loads[9:]:
         copy.wait()
@@ -271,6 +241,36 @@
     parts[side] = part_send[pl.ds(pl.multiple_of(side * 8, 8), 8), :]
     th[...], tl[...] = split(transfer_v[0])
 
+    buffers = ((kh0, kl0), (kh1, kl1))
+
+    def self_pair(t, carry):
+        for u in range(2):
+            leaf = t * 2 + u
+            for step in tile_pieces(spread, leaf, pts[HOME * LEAVES + leaf], *buffers[u]):
+                step()
+        for u in range(2):
+            leaf = t * 2 + u
+            high, low = buffers[u]
+            v = own_v[leaf]
+            own_sum[leaf] = folded(mul(v, high[...], NT) + mul(v, low[...], NT))
+        return carry
+
+    lax.fori_loop(0, LEAVES // 2, self_pair, 0)
+
+    for d in range(3):
+        spread_skel[d, :LEAVES * SKEL] = column_form(leaf_skel_v[d:d + 1, :], LEAVES * SKEL)
+        spread_skel[d, LEAVES * SKEL:] = column_form(parent_skel_v[d:d + 1, :], SKEL)
+    near_run[...] = jnp.zeros_like(near_run)
+    pairs = FAR_ROWS // 2
+    far_x[pairs * 8:, :] = jnp.zeros((512 - pairs * 8, 128), f32)
+    for u in range(2):
+        key_row = jnp.full((1, 128), -1, i32)
+        for j in range(pairs):
+            o, p = foff[0, far_base + 2 * j + u], fpart[far_base + 2 * j + u]
+            key = jnp.where(p < LEAVES, o * 8 + p, 8 * SPAN + o)
+            key_row = jnp.where((lanes == j) | (lanes == j + 64), key, key_row)
+        chosen_far[u * 64:(u + 1) * 64, :] = jnp.where(row_index((64, 128)) == key_row, 1.0, 0.0).astype(bf16)
+
     plan_copy.wait()
 
     def arrive(g):
@@ -359,11 +359,7 @@
             near_reply(t)
             reply_copy(t, t + 1).start()
 
-        @pl.when(t == 0)
-        def _():
-            send_table()
-
-        @pl.when(t == 2)
+        @pl.when(t == 1)
         def _():
             far_pairs()
 
@@ -471,6 +467,7 @@
         for o in (4, 5, 6, 2, 1, 0):
             far_copy(o).start()
 
+    send_table()
     for g in range(3):
         arrive(g)
     lax.fori_loop(0, 5, near_phase, jnp.zeros((COLS, LEAF), f32))
@@ -484,14 +481,6 @@
         for u in range(NEAR_PER):
             total = total + near_own[plan[2, leaf * NEAR_PER + u]]
         own_sum[leaf] = total
-    for g in AWAY:
-        reply_copy(g, 1).wait_recv()
-    for leaf in range(LEAVES):
-        total = own_sum[leaf]
-        for g in AWAY:
-            total = total + near_recv[g, leaf]
-        own_sum[leaf] = total
-
     for j in range(1, sides):
         interp_copy(j).wait_recv()
     for m in range(4):
@@ -517,8 +506,16 @@
         both = jnp.concatenate([stacked(jnp.where(left, even, zero)), stacked(jnp.where(left, zero, odd))], axis=0)
         got = mul(both, ih[m]) + mul(both, il[m])
         for u in range(2):
-            leaf = 2 * m + u
-            out[:, leaf * LEAF:(leaf + 1) * LEAF] = COUPLE * (own_sum[leaf] + folded(got[16 * u:16 * u + 16]))
+            own_sum[2 * m + u] = own_sum[2 * m + u] + folded(got[16 * u:16 * u + 16])
+
+    for g in AWAY:
+        reply_copy(g, 1).wait_recv()
+    for leaf in range(LEAVES):
+        total = own_sum[leaf]
+        for g in AWAY:
+            total = total + near_recv[g, leaf]
+        out[:, leaf * LEAF:(leaf + 1) * LEAF] = COUPLE * total
+
 
     for copy in mix_copies + data_copies + skel_copies + part_copies:
         copy.wait_send()

time: 41.5 us -> 40.1 us (0.966)
  Pallas kernels: 39.6 us -> 38.5 us
    pallas_call x1, Pallas kernels: 39.6 us -> 38.5 us  [shards(): pl.pallas_call(functools.partial(kernel, boxes, sides), out_shape=jax.Sha...]
where the time goes in v3:
time: 40.1 us; the launch traced here: 39.9 us
  Pallas kernels  38.5 us (96%)
  local copies, waits for them, and re-layouts  1.47 us (4%)
    pallas_call x1, Pallas kernels, shards(): pl.pallas_call(functools.partial(kernel, boxes, sides), out_shape=jax.Sha...  38.5 us
    unnamed x1, local copies, waits for them, and re-layouts  1.47 us

profile of v3, /device:TPU:1, one launch (start us, length us, event | category | flops | bytes accessed | tf_op | source)
XLA Modules:
  0.0 39.9 jit_solution(9332045363528723504)
XLA Ops:
  0.0 38.5 %shard_map.109 = f32[8,2048]{1,0:T(8,128)} custom-call(f32[3,2048]{1,0:T(4,128)} %coords.1, f32[8,2048]{1,0:T(8,128)} %charges.1, f32[3,512]{1,0:T(4,128)} %leaf_skel.1, f32[3,64]{1,0:T(4,128)} %parent_skel.1, f32[2,64,256]{2,1,0:T(8,128)} %interp.1, f32[1,64,512]{2,1,0:T(8,128)} %transfer.1, s32[1,5120]{1,0:T(1,128)} %bitcast.3, s32[5120]{0:T(1024)} %near_partner.1, ...), custom_call_target="tpu_custom_call" | custom-call | tf_op jit(solution)/shard_map/pallas_call | solution.py:541
  38.5 1.5 %copy.13 = f32[8,2048]{1,0:T(8,128)} copy(f32[8,2048]{1,0:T(8,128)} %shard_map.109) | data formatting | bytes 131072

commit v4 on v3

--- a/solution.py
+++ b/solution.py
@@ -9,9 +9,10 @@
 
 REACH = 3
 SPAN = 2 * REACH + 1
-ORDER = (4, 5, 6, 3, 2, 1, 0)
 HOME = 3
-AWAY = (0, 1, 2, 4, 5, 6)
+FIRST = (1, 2, 3, 0, -1, -2, -3)
+USUAL = (1, 3, -3, 0, 2, -2, -1)
+SENDS = (4, 6, 0, 5, 1, 2)
 SOFTEN = 0.0025
 COUPLE = 0.07957747154594767
 
@@ -108,6 +109,12 @@
     side = lax.axis_index("rhs")
     others = [o for o in range(SPAN) if o != REACH]
 
+    ends = (me < REACH) | (me >= boxes - REACH)
+    steps = [jnp.where(ends, FIRST[g], USUAL[g]) for g in range(SPAN)]
+
+    def step_from(g, t):
+        return jnp.where(t == 0, steps[g], jnp.where(t == 1, steps[g + 1], steps[g + 2]))
+
     def box_at(step):
         return lax.rem(me + (step + boxes), boxes)
 
@@ -134,8 +141,8 @@
         copy.wait()
     for leaf in range(LEAVES):
         at = slice(leaf * LEAF, (leaf + 1) * LEAF)
-        vals_in[HOME, leaf] = charges_v[:, at]
-        pts_in[HOME, leaf] = coords_v[:, at]
+        vals_in[REACH, leaf] = charges_v[:, at]
+        pts_in[REACH, leaf] = coords_v[:, at]
         vals[HOME * LEAVES + leaf] = charges_v[:, at]
         pts[HOME * LEAVES + leaf] = coords_v[:, at]
     skel[REACH, :, :512] = leaf_skel_v[...]
@@ -158,18 +165,18 @@
         for j in range(1, sides)
     ]
 
-    def data_copy(n, g, target):
+    def data_copy(n, o, target):
         src = (vals_in, pts_in)[n]
         return pltpu.make_async_remote_copy(
-            src_ref=src.at[HOME], dst_ref=src.at[g], send_sem=s_dat.at[n, g], recv_sem=r_dat.at[n, g],
+            src_ref=src.at[REACH], dst_ref=src.at[o], send_sem=s_dat.at[n, o], recv_sem=r_dat.at[n, o],
             device_id=target, device_id_type=MESH,
         )
 
     data_copies, skel_copies = [], []
-    for g in AWAY:
-        target = {"box": box_at(REACH - ORDER[g])}
+    for o in SENDS:
+        target = {"box": box_at(REACH - o)}
         for n in range(2):
-            copy = data_copy(n, g, target)
+            copy = data_copy(n, o, target)
             copy.start()
             data_copies.append(copy)
     for o in others:
@@ -189,10 +196,11 @@
     lanes = lane_index((1, 128))
     code = jnp.full((1, 128), 63 * 8, i32)
     for k in range(NEAR_ROWS):
-        hop = noff[0, near_base + k] - REACH
-        group = jnp.where(hop > 0, hop - 1, HOME - hop)
-        one = group * 64 + npart[near_base + k] * 8 + k // NEAR_PER + jnp.where(k < alive, 512, 0)
+        one = noff[0, near_base + k] * 64 + npart[near_base + k] * 8 + k // NEAR_PER + jnp.where(k < alive, 512, 0)
         code = jnp.where(lanes == k, one, code)
+    offset = (code >> 6) & 7
+    group = sum(jnp.where(offset == steps[g] + REACH, g, 0) for g in range(SPAN))
+    code = code + jnp.where(offset == SPAN, 0, group - offset) * 64
     code_col = column_form(code, 128)
     pair, pair_col = (code >> 3) & 63, (code_col >> 3) & 63
     key, key_col = pair * 128 + lanes, pair_col * 128 + row_index((128, 128))
@@ -273,13 +281,13 @@
 
     plan_copy.wait()
 
-    def arrive(g):
-        here = {"box": box_at(1)}
+    def arrive(g, step):
+        o = step + REACH
         for n in range(2):
-            data_copy(n, g, here).wait_recv()
+            data_copy(n, o, {"box": box_at(1)}).wait_recv()
         for leaf in range(LEAVES):
-            vals[g * LEAVES + leaf] = vals_in[g, leaf]
-            pts[g * LEAVES + leaf] = pts_in[g, leaf]
+            vals[g * LEAVES + leaf] = vals_in[o, leaf]
+            pts[g * LEAVES + leaf] = pts_in[o, leaf]
 
     def table_copy(g, step):
         slot = step + REACH
@@ -289,8 +297,9 @@
         )
 
     def reply_copy(g, step):
+        o = step + REACH
         return pltpu.make_async_remote_copy(
-            src_ref=near_send.at[g], dst_ref=near_recv.at[g], send_sem=s_near.at[g], recv_sem=r_near.at[g],
+            src_ref=near_send.at[g], dst_ref=near_recv.at[o], send_sem=s_near.at[o], recv_sem=r_near.at[o],
             device_id={"box": box_at(step)}, device_id_type=MESH,
         )
 
@@ -315,7 +324,7 @@
     def near_phase(t, run):
         @pl.when(t > 1)
         def _():
-            arrive(t + 2)
+            arrive(t + 2, step_from(4, t - 2))
 
         first = t * 16
         kept_run = [run]
@@ -357,9 +366,19 @@
         @pl.when(t < 3)
         def _():
             near_reply(t)
-            reply_copy(t, t + 1).start()
-
-        @pl.when(t == 1)
+            reply_copy(t, step_from(0, t)).start()
+
+        @pl.when((t == 0) & (me < REACH))
+        def _():
+            send_table()
+
+        @pl.when(t == 4)
+        def _():
+            for g in (4, 5, 6):
+                near_reply(g)
+                reply_copy(g, steps[g]).start()
+
+        @pl.when(t == 2)
         def _():
             far_pairs()
 
@@ -374,8 +393,8 @@
             if m:
                 total = total + parts[m, :, 128:256]
         tables[REACH, :, 512:640] = total
-        for g in AWAY:
-            table_copy(g, ORDER[g] - REACH).start()
+        for o in SENDS:
+            table_copy(0, o - REACH).start()
         for j in range(1, sides):
             interp_copy(j).start()
 
@@ -467,13 +486,13 @@
         for o in (4, 5, 6, 2, 1, 0):
             far_copy(o).start()
 
-    send_table()
+    @pl.when(me >= REACH)
+    def _():
+        send_table()
+
     for g in range(3):
-        arrive(g)
+        arrive(g, steps[g])
     lax.fori_loop(0, 5, near_phase, jnp.zeros((COLS, LEAF), f32))
-    for g in (4, 5, 6):
-        near_reply(g)
-        reply_copy(g, ORDER[g] - REACH).start()
     near_reply(HOME)
 
     for leaf in range(LEAVES):
@@ -508,12 +527,12 @@
         for u in range(2):
             own_sum[2 * m + u] = own_sum[2 * m + u] + folded(got[16 * u:16 * u + 16])
 
-    for g in AWAY:
-        reply_copy(g, 1).wait_recv()
+    for o in others:
+        reply_copy(0, o - REACH).wait_recv()
     for leaf in range(LEAVES):
         total = own_sum[leaf]
-        for g in AWAY:
-            total = total + near_recv[g, leaf]
+        for o in others:
+            total = total + near_recv[o, leaf]
         out[:, leaf * LEAF:(leaf + 1) * LEAF] = COUPLE * total
 
 
@@ -521,11 +540,10 @@
         copy.wait_send()
     for j in range(1, sides):
         interp_copy(j).wait_send()
-    for g in AWAY:
-        step = ORDER[g] - REACH
-        table_copy(g, step).wait_send()
-        reply_copy(g, step).wait_send()
-        far_copy(ORDER[g]).wait_send()
+    for o in others:
+        table_copy(0, o - REACH).wait_send()
+        reply_copy(0, o - REACH).wait_send()
+        far_copy(o).wait_send()
 
 
 def shards(

time: 40.1 us -> 39.6 us (0.988)
  Pallas kernels: 38.5 us -> 37.9 us
    pallas_call x1, Pallas kernels: 38.5 us -> 37.9 us  [shards(): pl.pallas_call(functools.partial(kernel, boxes, sides), out_shape=jax.Sha...]
where the time goes in v4:
time: 39.6 us; the launch traced here: 39.4 us
  Pallas kernels  37.9 us (96%)
  local copies, waits for them, and re-layouts  1.47 us (4%)
    pallas_call x1, Pallas kernels, shards(): pl.pallas_call(functools.partial(kernel, boxes, sides), out_shape=jax.Sha...  37.9 us
    unnamed x1, local copies, waits for them, and re-layouts  1.47 us

profile of v4, /device:TPU:1, one launch (start us, length us, event | category | flops | bytes accessed | tf_op | source)
XLA Modules:
  0.0 39.4 jit_solution(6610652700064877646)
XLA Ops:
  0.0 37.9 %shard_map.109 = f32[8,2048]{1,0:T(8,128)} custom-call(f32[3,2048]{1,0:T(4,128)} %coords.1, f32[8,2048]{1,0:T(8,128)} %charges.1, f32[3,512]{1,0:T(4,128)} %leaf_skel.1, f32[3,64]{1,0:T(4,128)} %parent_skel.1, f32[2,64,256]{2,1,0:T(8,128)} %interp.1, f32[1,64,512]{2,1,0:T(8,128)} %transfer.1, s32[1,5120]{1,0:T(1,128)} %bitcast.3, s32[5120]{0:T(1024)} %near_partner.1, ...), custom_call_target="tpu_custom_call" | custom-call | tf_op jit(solution)/shard_map/pallas_call | solution.py:559
  37.9 1.5 %copy.13 = f32[8,2048]{1,0:T(8,128)} copy(f32[8,2048]{1,0:T(8,128)} %shard_map.109) | data formatting | bytes 131072

commit v5 on v4

--- a/solution.py
+++ b/solution.py
@@ -381,6 +381,8 @@
         @pl.when(t == 2)
         def _():
             far_pairs()
+            for j in range(1, sides):
+                interp_copy(j).start()
 
         return kept_run[0]
 
@@ -395,8 +397,6 @@
         tables[REACH, :, 512:640] = total
         for o in SENDS:
             table_copy(0, o - REACH).start()
-        for j in range(1, sides):
-            interp_copy(j).start()
 
     def far_pairs():
         for copy in skel_copies:

time: 39.6 us -> 39.6 us (level)
  no operation moved by 1% of the time
where the time goes in v5:
time: 39.6 us; the launch traced here: 39.4 us
  Pallas kernels  37.9 us (96%)
  local copies, waits for them, and re-layouts  1.47 us (4%)
    pallas_call x1, Pallas kernels, shards(): pl.pallas_call(functools.partial(kernel, boxes, sides), out_shape=jax.Sha...  37.9 us
    unnamed x1, local copies, waits for them, and re-layouts  1.47 us

profile of v5, /device:TPU:1, one launch (start us, length us, event | category | flops | bytes accessed | tf_op | source)
XLA Modules:
  0.0 39.4 jit_solution(12690820316997905495)
XLA Ops:
  0.0 37.9 %shard_map.109 = f32[8,2048]{1,0:T(8,128)} custom-call(f32[3,2048]{1,0:T(4,128)} %coords.1, f32[8,2048]{1,0:T(8,128)} %charges.1, f32[3,512]{1,0:T(4,128)} %leaf_skel.1, f32[3,64]{1,0:T(4,128)} %parent_skel.1, f32[2,64,256]{2,1,0:T(8,128)} %interp.1, f32[1,64,512]{2,1,0:T(8,128)} %transfer.1, s32[1,5120]{1,0:T(1,128)} %bitcast.3, s32[5120]{0:T(1024)} %near_partner.1, ...), custom_call_target="tpu_custom_call" | custom-call | tf_op jit(solution)/shard_map/pallas_call | solution.py:559
  37.9 1.5 %copy.13 = f32[8,2048]{1,0:T(8,128)} copy(f32[8,2048]{1,0:T(8,128)} %shard_map.109) | data formatting | bytes 131072
